TPU v7x, 32 devices: a whole 2x2x4 slice. The times are simulated.
32 devices in a mesh: seq: 8 (over z, y), head: 4 (over x, core).
Axes of the slice: x: 2, y: 2, z: 4, core: 2. Of those that a mesh axis runs over, the one named last changes fastest.
Arguments:
- queries: bfloat16 [1024, 2048], P('seq', 'head'), may hold values from -6 to 6
- keys: bfloat16 [1024, 2048], P('seq', 'head'), may hold values from -6 to 6
- values: bfloat16 [1024, 2048], P('seq', 'head'), may hold values from -6 to 6
- grad_out: bfloat16 [1024, 2048], P('seq', 'head'), may hold values from -6 to 6
- gain: float32 [2048], P('head'), may hold values from 0.1 to 1.9
- segment_ids: int32 [8, 128], P('seq'), may hold values from 0 to 7, never falling along the last dimension, each value on 1 to 32 neighbouring positions
Outputs:
- output: bfloat16 [1024, 2048], P('seq', 'head')
- grad_queries: bfloat16 [1024, 2048], P('seq', 'head')
- grad_keys: bfloat16 [1024, 2048], P('seq', 'head')
- grad_values: bfloat16 [1024, 2048], P('seq', 'head')
Inputs may be any that keep to these rules, and one draw needn't show every extreme that they name: `segment_ids`: ids never fall along a group; each mask block holds 1 to 32 tokens, one exactly 32.
All inputs are finite; a program needn't handle non-finite values.
Results may differ from a plain program's by a relative error of at most 0.0058.
Values sent between devices are 32-bit elements; how exact they have to be, the bound alone decides.
A program may use at most 64 MiB of HBM per device.

v0:
```python
import jax
import jax.numpy as jnp
from jax import lax
from jax.sharding import PartitionSpec as P

HD = 128
D = 2048


def carried_in(value, axis, combine, identity):
    count, position = (lax.axis_size(axis), lax.axis_index(axis))
    everything = lax.all_gather(value, axis)
    start = jnp.broadcast_to(jnp.asarray(identity, value.dtype), value.shape)

    def turn(k, before):
        reached = k < position
        new = combine(before, everything[k])
        return jnp.where(reached, new, before)

    return lax.fori_loop(0, count, turn, start)


def add_states(earlier, later_term):
    return earlier + later_term


def on_device(queries, keys, values, grad_out, gain, segment_ids):
    length = queries.shape[0]
    width = queries.shape[1]
    heads_here = width // HD
    queries_h = queries.reshape(length, heads_here, HD)
    keys_h = keys.reshape(length, heads_here, HD)
    values_h = values.reshape(length, heads_here, HD)
    segment = segment_ids[0]
    row_ids = lax.broadcasted_iota(jnp.int32, (length, length), 0)
    col_ids = lax.broadcasted_iota(jnp.int32, (length, length), 1)
    allowed = jnp.where(
        (segment[:, None] == segment[None, :]) & (col_ids <= row_ids), 1.0, 0.0
    ).astype(jnp.float32)
    raw_scores = jnp.einsum("thd,shd->hts", queries_h, keys_h, preferred_element_type=jnp.float32)
    scores = (raw_scores * allowed[None]).astype(jnp.bfloat16)
    local_state = jnp.einsum("thd,the->hde", keys_h, values_h, preferred_element_type=jnp.float32)
    zero_state = jnp.zeros_like(local_state)
    state = carried_in(local_state, "seq", add_states, zero_state)
    state_b = state.astype(jnp.bfloat16)
    attn = jnp.einsum("hts,she->the", scores, values_h, preferred_element_type=jnp.float32)
    attn = attn + jnp.einsum("thd,hde->the", queries_h, state_b, preferred_element_type=jnp.float32)
    flat = attn.reshape(length, width)
    gained = gain * grad_out.astype(jnp.float32)
    squares, products = lax.psum(
        (jnp.sum(flat * flat, axis=1), jnp.sum(gained * flat, axis=1)), "head"
    )
    inverse = lax.rsqrt(squares / D + 1e-06)
    output = (gain * flat * inverse[:, None]).astype(jnp.bfloat16)
    dflat = gained * inverse[:, None] - flat * (products * inverse**3 / D)[:, None]
    dattn = dflat.astype(jnp.bfloat16).reshape(length, heads_here, HD)
    grad_local = jnp.einsum("thd,the->hde", queries_h, dattn, preferred_element_type=jnp.float32)
    overall = lax.psum(grad_local, "seq")
    before = carried_in(grad_local, "seq", add_states, zero_state)
    later = overall - before - grad_local
    later_b = later.astype(jnp.bfloat16)
    dscores = (
        jnp.einsum("the,she->hts", dattn, values_h, preferred_element_type=jnp.float32)
        * allowed[None]
    ).astype(jnp.bfloat16)
    grad_q = jnp.einsum("hts,shd->thd", dscores, keys_h, preferred_element_type=jnp.float32)
    grad_q = grad_q + jnp.einsum("the,hde->thd", dattn, state_b, preferred_element_type=jnp.float32)
    grad_k = jnp.einsum("hts,thd->shd", dscores, queries_h, preferred_element_type=jnp.float32)
    grad_k = grad_k + jnp.einsum(
        "she,hde->shd", values_h, later_b, preferred_element_type=jnp.float32
    )
    grad_v = jnp.einsum("hts,the->she", scores, dattn, preferred_element_type=jnp.float32)
    grad_v = grad_v + jnp.einsum(
        "shd,hde->she", keys_h, later_b, preferred_element_type=jnp.float32
    )
    return (
        output,
        grad_q.reshape(length, width).astype(jnp.bfloat16),
        grad_k.reshape(length, width).astype(jnp.bfloat16),
        grad_v.reshape(length, width).astype(jnp.bfloat16),
    )


def solution(mesh):
    placed = (
        P("seq", "head"),
        P("seq", "head"),
        P("seq", "head"),
        P("seq", "head"),
        P("head"),
        P("seq", None),
    )
    return jax.shard_map(
        on_device,
        mesh=mesh,
        in_specs=placed,
        out_specs=(P("seq", "head"), P("seq", "head"), P("seq", "head"), P("seq", "head")),
        check_vma=False,
    )
```

profile of v0, /device:TPU:0, one launch (start us, length us, event | category | flops | bytes accessed | tf_op | source)
XLA Modules:
  0.0 209.4 jit_solution(17428342165061876624)
XLA Ops:
  7.2 1.1 copy.108
  8.3 1.8 fusion.11
  11.0 1.1 fusion.5
  12.1 1.1 convolution_bitcast_fusion.6
  13.3 49.0 %all-gather.5.cloned.1.call-done = f32[32,128,128]{2,1,0:T(8,128)} async-done(((f32[4,128,128]{2,1,0:T(8,128)}), f32[32,128,128]{2,1,0:T(8,128)}) %all-gather.5.cloned.1.call-update) | async-done | bytes 2097168 | tf_op jit(solution)/shard_map/all_gather | solution.py:12
  62.2 8.5 %while.28 = (s32[]{:T(128)}, f32[4,128,128]{2,1,0:T(8,128)S(1)}, s32[]{:T(128)}, f32[8,4,128,128]{3,2,1,0:T(8,128)}, s32[]{:T(128)}, /*index=5*/s32[]{:T(128)}) while((s32[]{:T(128)}, f32[4,128,128]{2,1,0:T(8,128)S(1)}, s32[]{:T(128)}, f32[8,4,128,128]{3,2,1,0:T(8,128)}, s32[]{:T(128)}, /*index=5*/s32[]{:T(128)}) %tuple.82), condition=%wide.region_1.2_spmd.clone, body=%wide.region_0.1_spmd.clone.sunk | while | flops 196612 | bytes 786533 | solution.py:20
  62.2 1.1 add_select_fusion.4
  63.3 1.0 add_select_fusion.4
  64.4 1.0 add_select_fusion.4
  65.5 1.0 add_select_fusion.4
  66.5 1.0 add_select_fusion.4
  67.6 1.0 add_select_fusion.4
  68.7 1.0 add_select_fusion.4
  69.7 1.0 add_select_fusion.4
  71.3 5.7 %all-reduce = (f32[128]{0:T(128)S(1)}, f32[128]{0:T(128)S(1)}) all-reduce(f32[128]{0:T(128)S(1)} %get-tuple-element.228, f32[128]{0:T(128)S(1)} %multiply_reduce_fusion), channel_id=1, replica_groups=mesh['seq'=8,'head'=4] {'head'}, use_global_device_ids=true, to_apply=%region_3.4 | all-reduce | flops 256 | bytes 2048 | tf_op jit(solution)/shard_map/psum | solution.py:50
  80.7 46.5 %all-gather.7.cloned.1.call-done = f32[32,128,128]{2,1,0:T(8,128)} async-done(((f32[4,128,128]{2,1,0:T(8,128)}), f32[32,128,128]{2,1,0:T(8,128)}) %all-gather.7.cloned.1.call-update) | async-done | bytes 2097168 | tf_op jit(solution)/shard_map/all_gather | solution.py:12
  127.2 8.6 %while.29 = (s32[]{:T(128)}, f32[4,128,128]{2,1,0:T(8,128)S(1)}, s32[]{:T(128)}, f32[8,4,128,128]{3,2,1,0:T(8,128)}, s32[]{:T(128)}, /*index=5*/s32[]{:T(128)}) while((s32[]{:T(128)}, f32[4,128,128]{2,1,0:T(8,128)S(1)}, s32[]{:T(128)}, f32[8,4,128,128]{3,2,1,0:T(8,128)}, s32[]{:T(128)}, /*index=5*/s32[]{:T(128)}) %tuple.81), condition=%wide.region_8.9_spmd.clone, body=%wide.region_7.8_spmd.clone.sunk | while | flops 196612 | bytes 786533 | solution.py:20
  127.2 1.1 add_select_fusion.5
  128.3 1.0 add_select_fusion.5
  129.3 1.0 add_select_fusion.5
  130.4 1.0 add_select_fusion.5
  133.6 1.1 add_select_fusion.5
  134.7 1.0 add_select_fusion.5
  135.9 63.7 %all-reduce.3.cloned.1.call-done = f32[4,128,128]{1,2,0:T(8,128)} async-done(((f32[4,128,128]{1,2,0:T(8,128)}), f32[4,128,128]{1,2,0:T(8,128)}) %all-reduce.3.cloned.1.call-update) | async-done | bytes 262160 | tf_op jit(solution)/shard_map/psum | solution.py:58
  (45 shorter events, 10.4 us)
Async XLA Ops:
  7.2 3.8 %copy-start = (bf16[128,512]{1,0:T(8,128)(2,1)S(1)}, bf16[128,512]{1,0:T(8,128)(2,1)}, u32[]{:S(2)}) copy-start(bf16[128,512]{1,0:T(8,128)(2,1)} %param.10) | copy-start | bytes 393220
  7.2 55.1 %all-gather.5.cloned.1.call-start = ((), (), s32[]{:S(2)}) async-start(), calls=%async_computation.1 | async-start | bytes 2359296 | tf_op jit(solution)/shard_map/all_gather | solution.py:12
  10.1 117.1 %all-gather.7.cloned.1.call-start = ((), (), s32[]{:S(2)}) async-start(), calls=%async_computation.2 | async-start | bytes 2359296 | tf_op jit(solution)/shard_map/all_gather | solution.py:12
  62.2 9.0 %copy-start.5 = (bf16[128,512]{1,0:T(8,128)(2,1)S(1)}, bf16[128,512]{1,0:T(8,128)(2,1)}, u32[]{:S(2)}) copy-start(bf16[128,512]{1,0:T(8,128)(2,1)} %param.13) | copy-start | bytes 393220
  62.2 9.0 %copy-start.6 = (f32[512]{0:T(512)S(1)}, f32[512]{0:T(512)}, u32[]{:S(2)}) copy-start(f32[512]{0:T(512)} %param.14) | copy-start | bytes 6148
  70.8 8.2 %copy-start.3 = (bf16[128,512]{1,0:T(8,128)(2,1)S(1)}, bf16[128,512]{1,0:T(8,128)(2,1)}, u32[]{:S(2)}) copy-start(bf16[128,512]{1,0:T(8,128)(2,1)} %param.12) | copy-start | bytes 393220
  78.1 2.5 %copy-start.1 = (f32[4,128,128]{1,2,0:T(8,128)}, f32[4,128,128]{1,2,0:T(8,128)S(1)}, u32[]{:S(2)}) copy-start(f32[4,128,128]{1,2,0:T(8,128)S(1)} %convolution_bitcast_fusion.2) | copy-start | bytes 786436
  79.0 120.6 %all-reduce.3.cloned.1.call-start = ((), (), s32[]{:S(2)}) async-start(), calls=%async_computation | async-start | bytes 524288 | tf_op jit(solution)/shard_map/psum | solution.py:58
  127.2 72.4 %copy-start.2 = (f32[4,128,128]{1,2,0:T(8,128)S(1)}, f32[4,128,128]{1,2,0:T(8,128)}, u32[]{:S(2)}) copy-start(f32[4,128,128]{1,2,0:T(8,128)} %copy-done.1) | copy-start | bytes 786436
  127.2 73.7 %copy-start.4 = (bf16[128,512]{1,0:T(8,128)(2,1)S(1)}, bf16[128,512]{1,0:T(8,128)(2,1)}, u32[]{:S(2)}) copy-start(bf16[128,512]{1,0:T(8,128)(2,1)} %param.11) | copy-start | bytes 393220
Sparse Core Ops, SparseCore 0:
  10.2 51.9 all-gather.4
  79.1 48.0 all-gather.6
  130.5 69.0 all-reduce.2
where the time goes:
time: 210 us; the launch traced here: 209 us
  waiting for transfers between devices  159 us (76%)
  other arithmetic  19.5 us (9%)
  between operations  14 us (7%)
  matrix products  5.95 us (3%)
  blocking collectives  5.66 us (3%)
  local copies, waits for them, and re-layouts  4.61 us (2%)
    all_gather x2, waiting for transfers between devices, carried_in(): everything = lax.all_gather(value, axis)  95.5 us
    psum x1, waiting for transfers between devices, on_device(): overall = lax.psum(grad_local, 'seq')  63.7 us
    select_n x16, other arithmetic, turn(): return jnp.where(reached, new, before)  16.7 us
    psum x1, blocking collectives, on_device(): lax.psum((jnp.sum(flat * flat, axis=1), jnp.sum(gained * flat, axis=1)),...  5.66 us
  transfers between devices with their start and end apart: 3, of which 3 were waited for; matrix products, arithmetic and copies ran while one was open for 6% of the time, Pallas kernels for 0%

commit v1 on v0

v1 whole, which is shorter than its diff:
```python
import functools

import jax
import jax.numpy as jnp
from jax import lax
from jax.experimental import pallas as pl
from jax.experimental.pallas import tpu as pltpu
from jax.sharding import PartitionSpec as P

HD = 128
INNER = 2
PARTS = 2
MESH = pl.DeviceIdType.MESH
F32 = jnp.float32
BF16 = jnp.bfloat16


def dot(a, b, dims):
    return lax.dot_general(a, b, (dims, ((), ())), preferred_element_type=F32)


NN = ((1,), (0,))
NT = ((1,), (1,))
TN = ((0,), (0,))


def kernel(
    n_seq, n_head, heads, q_ref, k_ref, v_ref, dy_ref, gain_ref, seg_ref,
    out_ref, gq_ref, gk_ref, gv_ref,
    own, zin, yin, scores, state_b, attn, dattn, part_k, part_v, norm_out, norm_in,
    zs, zr, ys, yr, ns, nr,
):
    length = q_ref.shape[0]
    features = n_head * heads * HD
    rows = HD // PARTS
    chunks = heads * PARTS
    s, h = lax.axis_index("seq"), lax.axis_index("head")
    y, z = lax.rem(s, INNER), s // INNER
    depth = n_seq // INNER
    across = s + 1 - 2 * y
    bottom, top = z == 0, z == depth - 1
    inner = jnp.logical_not(bottom), jnp.logical_not(top)

    def cols(i):
        return slice(i * HD, (i + 1) * HD)

    def peer(k):
        return lax.rem(h + k, n_head)

    barrier = pltpu.get_barrier_semaphore()
    pl.semaphore_signal(barrier, inc=1, device_id=(across, h), device_id_type=MESH)
    for k in range(1, n_head):
        pl.semaphore_signal(barrier, inc=1, device_id=(s, peer(k)), device_id_type=MESH)

    @pl.when(inner[0])
    def _():
        pl.semaphore_signal(barrier, inc=1, device_id=(s - INNER, h), device_id_type=MESH)

    @pl.when(inner[1])
    def _():
        pl.semaphore_signal(barrier, inc=1, device_id=(s + INNER, h), device_id_type=MESH)

    starts = (bottom, top)
    ends = (top, bottom)
    nexts = (s + INNER, s - INNER)
    gives_all = (y == 0, y == 1)

    def hop(p, c):
        return pltpu.make_async_remote_copy(
            src_ref=own.at[p, c], dst_ref=zin.at[p, c], send_sem=zs.at[p, c],
            recv_sem=zr.at[p, c], device_id=(nexts[p], h), device_id_type=MESH,
        )

    def cross(p, c, src):
        return pltpu.make_async_remote_copy(
            src_ref=src.at[p, c], dst_ref=yin.at[p, c], send_sem=ys.at[p, c],
            recv_sem=yr.at[p, c], device_id=(across, h), device_id_type=MESH,
        )

    def keep(p, i, term):
        for j in range(PARTS):
            own[p, i * PARTS + j] = term[j * rows:(j + 1) * rows]

    def send_first(p):
        @pl.when(starts[p])
        def _():
            for c in range(chunks):
                hop(p, c).start()

                @pl.when(gives_all[p])
                def _():
                    cross(p, c, own).start()

    def clear(p):
        @pl.when(starts[p])
        def _():
            zin[p] = jnp.zeros(zin.shape[1:], F32)

            @pl.when(gives_all[p])
            def _():
                yin[p] = jnp.zeros(yin.shape[1:], F32)

    def carry_on(p):
        @pl.when(jnp.logical_not(starts[p]))
        def _():
            for c in range(chunks):
                hop(p, c).wait_recv()

                @pl.when(jnp.logical_not(gives_all[p]))
                def _():
                    cross(p, c, zin).start()

                own[p, c] = own[p, c] + zin[p, c]

                @pl.when(jnp.logical_not(ends[p]))
                def _():
                    hop(p, c).start()

                @pl.when(gives_all[p])
                def _():
                    cross(p, c, own).start()

    def carried(p, i):
        @pl.when(jnp.logical_not(starts[p] & gives_all[p]))
        def _():
            for j in range(PARTS):
                cross(p, i * PARTS + j, own).wait_recv()

        pieces = [zin[p, i * PARTS + j] + yin[p, i * PARTS + j] for j in range(PARTS)]
        return jnp.concatenate(pieces, axis=0).astype(BF16)

    def drain(p):
        for c in range(chunks):
            @pl.when(jnp.logical_not(ends[p]))
            def _():
                hop(p, c).wait_send()

            @pl.when(gives_all[p] | jnp.logical_not(starts[p]))
            def _():
                cross(p, c, own).wait_send()

    for i in range(heads):
        keep(0, i, dot(k_ref[:, cols(i)], v_ref[:, cols(i)], TN))

    pl.semaphore_wait(barrier, n_head + inner[0].astype(jnp.int32) + inner[1].astype(jnp.int32))
    send_first(0)
    clear(0)
    clear(1)

    along = jnp.broadcast_to(seg_ref[...], (length, length))
    row_ids = lax.broadcasted_iota(jnp.int32, (length, length), 0)
    col_ids = lax.broadcasted_iota(jnp.int32, (length, length), 1)
    allowed = (along.T == along) & (col_ids <= row_ids)
    for i in range(heads):
        raw = dot(q_ref[:, cols(i)], k_ref[:, cols(i)], NT)
        scores[i] = jnp.where(allowed, raw, 0.0).astype(BF16)
        attn[:, cols(i)] = dot(scores[i], v_ref[:, cols(i)], NN)

    carry_on(0)

    squares = jnp.zeros((length, HD), F32)
    products = jnp.zeros((length, HD), F32)
    for i in range(heads):
        state_b[i] = carried(0, i)
        flat = attn[:, cols(i)] + dot(q_ref[:, cols(i)], state_b[i], NN)
        attn[:, cols(i)] = flat
        gained = gain_ref[:, cols(i)] * dy_ref[:, cols(i)].astype(F32)
        squares = squares + flat * flat
        products = products + gained * flat

    norm_out[0:1] = jnp.sum(squares.T, axis=0, keepdims=True)
    norm_out[1:2] = jnp.sum(products.T, axis=0, keepdims=True)
    norm_out[2:8] = jnp.zeros((6, length), F32)

    def share(k):
        return pltpu.make_async_remote_copy(
            src_ref=norm_out, dst_ref=norm_in.at[k - 1], send_sem=ns.at[k - 1],
            recv_sem=nr.at[k - 1], device_id=(s, peer(k)), device_id_type=MESH,
        )

    for k in range(1, n_head):
        share(k).start()
    total = norm_out[...]
    for k in range(1, n_head):
        share(k).wait_recv()
        total = total + norm_in[k - 1]
    inverse_row = lax.rsqrt(total[0:1] / features + 1e-06)
    beta_row = total[1:2] * (inverse_row * inverse_row * inverse_row) / features
    inverse = jnp.broadcast_to(inverse_row, (HD, length)).T
    beta = jnp.broadcast_to(beta_row, (HD, length)).T

    for i in range(heads):
        gained = gain_ref[:, cols(i)] * dy_ref[:, cols(i)].astype(F32)
        dattn[i] = (gained * inverse - attn[:, cols(i)] * beta).astype(BF16)
        keep(1, i, dot(q_ref[:, cols(i)], dattn[i], TN))
    send_first(1)

    for i in range(heads):
        raw = dot(dattn[i], v_ref[:, cols(i)], NT)
        dscores = jnp.where(allowed, raw, 0.0).astype(BF16)
        gq = dot(dscores, k_ref[:, cols(i)], NN) + dot(dattn[i], state_b[i], NT)
        gq_ref[:, cols(i)] = gq.astype(BF16)
        part_k[i] = dot(dscores, q_ref[:, cols(i)], TN)
        part_v[i] = dot(scores[i], dattn[i], TN)
        out = gain_ref[:, cols(i)] * attn[:, cols(i)] * inverse
        out_ref[:, cols(i)] = out.astype(BF16)

    carry_on(1)

    for i in range(heads):
        later_b = carried(1, i)
        gk = part_k[i] + dot(v_ref[:, cols(i)], later_b, NT)
        gk_ref[:, cols(i)] = gk.astype(BF16)
        gv = part_v[i] + dot(k_ref[:, cols(i)], later_b, NN)
        gv_ref[:, cols(i)] = gv.astype(BF16)

    drain(0)
    drain(1)
    for k in range(1, n_head):
        share(k).wait_send()


def on_device(n_seq, n_head, queries, keys, values, grad_out, gain, segment_ids):
    length, width = queries.shape
    heads = width // HD
    chunks = heads * PARTS
    vmem = pl.BlockSpec(memory_space=pltpu.VMEM)
    states = pltpu.VMEM((2, chunks, HD // PARTS, HD), F32)
    return pl.pallas_call(
        functools.partial(kernel, n_seq, n_head, heads),
        out_shape=[jax.ShapeDtypeStruct((length, width), BF16)] * 4,
        in_specs=[vmem] * 6,
        out_specs=[vmem] * 4,
        scratch_shapes=[
            states,
            states,
            states,
            pltpu.VMEM((heads, length, length), BF16),
            pltpu.VMEM((heads, HD, HD), BF16),
            pltpu.VMEM((length, width), F32),
            pltpu.VMEM((heads, length, HD), BF16),
            pltpu.VMEM((heads, length, HD), F32),
            pltpu.VMEM((heads, length, HD), F32),
            pltpu.VMEM((8, length), F32),
            pltpu.VMEM((n_head - 1, 8, length), F32),
            pltpu.SemaphoreType.DMA((2, chunks)),
            pltpu.SemaphoreType.DMA((2, chunks)),
            pltpu.SemaphoreType.DMA((2, chunks)),
            pltpu.SemaphoreType.DMA((2, chunks)),
            pltpu.SemaphoreType.DMA((n_head - 1,)),
            pltpu.SemaphoreType.DMA((n_head - 1,)),
        ],
        compiler_params=pltpu.CompilerParams(
            collective_id=0, has_side_effects=True, vmem_limit_bytes=32 * 1024 * 1024
        ),
    )(queries, keys, values, grad_out, gain.reshape(1, width), segment_ids)


def solution(mesh):
    sizes = dict(mesh.shape)
    placed = P("seq", "head")
    return jax.shard_map(
        functools.partial(on_device, sizes["seq"], sizes["head"]),
        mesh=mesh,
        in_specs=(placed, placed, placed, placed, P("head"), P("seq", None)),
        out_specs=(placed,) * 4,
        check_vma=False,
    )
```

time: 210 us -> 48 us (0.23)
  waiting for transfers between devices: 159 us -> 0 us
  Pallas kernels: 0 us -> 39.6 us
  other arithmetic: 19.5 us -> 0 us
  between operations: 14 us -> 0.66 us
  matrix products: 5.95 us -> 0 us
  blocking collectives: 5.66 us -> 0 us
  local copies, waits for them, and re-layouts: 4.61 us -> 7.57 us
    all_gather x2 -> x0, waiting for transfers between devices: 95.5 us -> none  [carried_in(): everything = lax.all_gather(value, axis)]
    psum x1 -> x0, waiting for transfers between devices: 63.7 us -> none  [on_device(): overall = lax.psum(grad_local, 'seq')]
    pallas_call x0 -> x1, Pallas kernels: none -> 39.6 us  [on_device(): pl.pallas_call(functools.partial(kernel, n_seq, n_head, heads), out_shape...]
    select_n x17 -> x0, other arithmetic: 17.6 us -> none  [the longest x16 16.7 us: turn(): return jnp.where(reached, new, before)]
    dot_general x12 -> x0, matrix products: 5.95 us -> none  [the longest x1 1.78 us: on_device(): jnp.einsum('thd,the->hde', keys_h, values_h, preferred_element_type=jnp.f...]
    psum x1 -> x0, blocking collectives: 5.66 us -> none  [on_device(): lax.psum((jnp.sum(flat * flat, axis=1), jnp.sum(gained * flat, axis=1)),...]
    unnamed x17 -> x16, local copies, waits for them, and re-layouts: 2.35 us -> 7.57 us
  transfers between devices with their start and end apart: 3 -> 0, of which waited for: 3 -> 0; matrix products, arithmetic and copies ran while one was open for 6% -> 0% of each run, Pallas kernels for 0% -> 0%
where the time goes in v1:
time: 48 us; the launch traced here: 47.8 us
  Pallas kernels  39.6 us (82%)
  local copies, waits for them, and re-layouts  7.57 us (16%)
  between operations  0.66 us (1%)
    pallas_call x1, Pallas kernels, on_device(): pl.pallas_call(functools.partial(kernel, n_seq, n_head, heads), out_shape...  39.6 us
    unnamed x16, local copies, waits for them, and re-layouts  7.57 us

profile of v1, /device:TPU:0, one launch (start us, length us, event | category | flops | bytes accessed | tf_op | source)
XLA Modules:
  0.0 47.8 jit_solution(623211067222371221)
XLA Ops:
  0.6 0.0 copy-start.5
  0.6 0.6 %copy-done.5 = s32[1,128]{1,0:T(1,128)S(1)} copy-done((s32[1,128]{1,0:T(1,128)S(1)}, s32[1,128]{1,0:T(1,128)}, u32[]{:S(2)}) %copy-start.5) | copy-done | bytes 536
  1.3 0.0 copy-start
  1.3 0.9 %copy-done = bf16[128,512]{1,0:T(8,128)(2,1)S(1)} copy-done((bf16[128,512]{1,0:T(8,128)(2,1)S(1)}, bf16[128,512]{1,0:T(8,128)(2,1)}, u32[]{:S(2)}) %copy-start) | copy-done | bytes 131096
  2.2 0.0 copy-start.1
  2.2 0.9 %copy-done.1 = bf16[128,512]{1,0:T(8,128)(2,1)S(1)} copy-done((bf16[128,512]{1,0:T(8,128)(2,1)S(1)}, bf16[128,512]{1,0:T(8,128)(2,1)}, u32[]{:S(2)}) %copy-start.1) | copy-done | bytes 131096
  3.1 0.0 copy-start.2
  3.1 0.9 %copy-done.2 = bf16[128,512]{1,0:T(8,128)(2,1)S(1)} copy-done((bf16[128,512]{1,0:T(8,128)(2,1)S(1)}, bf16[128,512]{1,0:T(8,128)(2,1)}, u32[]{:S(2)}) %copy-start.2) | copy-done | bytes 131096
  4.0 0.0 copy-start.3
  4.0 0.9 %copy-done.3 = bf16[128,512]{1,0:T(8,128)(2,1)S(1)} copy-done((bf16[128,512]{1,0:T(8,128)(2,1)S(1)}, bf16[128,512]{1,0:T(8,128)(2,1)}, u32[]{:S(2)}) %copy-start.3) | copy-done | bytes 131096
  4.9 0.0 copy-start.4
  4.9 0.7 %copy-done.4 = f32[512]{0:T(512)S(1)} copy-done((f32[512]{0:T(512)S(1)}, f32[512]{0:T(512)}, u32[]{:S(2)}) %copy-start.4) | copy-done | bytes 2072
  5.6 39.6 %shard_map.93 = (bf16[128,512]{1,0:T(8,128)(2,1)S(1)}, bf16[128,512]{1,0:T(8,128)(2,1)S(1)}, bf16[128,512]{1,0:T(8,128)(2,1)S(1)}, bf16[128,512]{1,0:T(8,128)(2,1)S(1)}) custom-call(bf16[128,512]{1,0:T(8,128)(2,1)S(1)} %copy-done, bf16[128,512]{1,0:T(8,128)(2,1)S(1)} %copy-done.1, bf16[128,512]{1,0:T(8,128)(2,1)S(1)} %copy-done.2, ...), custom_call_target="tpu_custom_call" | custom-call | tf_op jit(solution)/shard_map/pallas_call | solution.py:229
  45.2 0.7 %copy.14 = bf16[128,512]{1,0:T(8,128)(2,1)} copy(bf16[128,512]{1,0:T(8,128)(2,1)S(1)} %get-tuple-element.8) | data formatting | bytes 262144
  45.8 0.7 %copy.15 = bf16[128,512]{1,0:T(8,128)(2,1)} copy(bf16[128,512]{1,0:T(8,128)(2,1)S(1)} %get-tuple-element.9) | data formatting | bytes 262144
  46.5 0.7 %copy.16 = bf16[128,512]{1,0:T(8,128)(2,1)} copy(bf16[128,512]{1,0:T(8,128)(2,1)S(1)} %get-tuple-element.10) | data formatting | bytes 262144
  47.2 0.7 %copy.17 = bf16[128,512]{1,0:T(8,128)(2,1)} copy(bf16[128,512]{1,0:T(8,128)(2,1)S(1)} %get-tuple-element.11) | data formatting | bytes 262144
Async XLA Ops:
  0.6 0.7 %copy-start.5 = (s32[1,128]{1,0:T(1,128)S(1)}, s32[1,128]{1,0:T(1,128)}, u32[]{:S(2)}) copy-start(s32[1,128]{1,0:T(1,128)} %seg_ref.1) | copy-start | bytes 1540
  1.3 0.9 %copy-start = (bf16[128,512]{1,0:T(8,128)(2,1)S(1)}, bf16[128,512]{1,0:T(8,128)(2,1)}, u32[]{:S(2)}) copy-start(bf16[128,512]{1,0:T(8,128)(2,1)} %q_ref.1) | copy-start | bytes 393220
  2.2 0.9 %copy-start.1 = (bf16[128,512]{1,0:T(8,128)(2,1)S(1)}, bf16[128,512]{1,0:T(8,128)(2,1)}, u32[]{:S(2)}) copy-start(bf16[128,512]{1,0:T(8,128)(2,1)} %k_ref.1) | copy-start | bytes 393220
  3.1 0.9 %copy-start.2 = (bf16[128,512]{1,0:T(8,128)(2,1)S(1)}, bf16[128,512]{1,0:T(8,128)(2,1)}, u32[]{:S(2)}) copy-start(bf16[128,512]{1,0:T(8,128)(2,1)} %v_ref.1) | copy-start | bytes 393220
  4.0 0.9 %copy-start.3 = (bf16[128,512]{1,0:T(8,128)(2,1)S(1)}, bf16[128,512]{1,0:T(8,128)(2,1)}, u32[]{:S(2)}) copy-start(bf16[128,512]{1,0:T(8,128)(2,1)} %dy_ref.1) | copy-start | bytes 393220
  4.9 0.7 %copy-start.4 = (f32[512]{0:T(512)S(1)}, f32[512]{0:T(512)}, u32[]{:S(2)}) copy-start(f32[512]{0:T(512)} %param.10) | copy-start | bytes 6148

commit v2 on v1

--- a/solution.py
+++ b/solution.py
@@ -10,6 +10,7 @@
 HD = 128
 INNER = 2
 PARTS = 2
+VMEM = 65000 * 1024
 MESH = pl.DeviceIdType.MESH
 F32 = jnp.float32
 BF16 = jnp.bfloat16
@@ -25,15 +26,16 @@
 
 
 def kernel(
-    n_seq, n_head, heads, q_ref, k_ref, v_ref, dy_ref, gain_ref, seg_ref,
+    n_seq, n_head, heads, direct, rows, q_hbm, k_hbm, v_hbm, dy_hbm, gain_hbm, seg_hbm,
     out_ref, gq_ref, gk_ref, gv_ref,
-    own, zin, yin, scores, state_b, attn, dattn, part_k, part_v, norm_out, norm_in,
-    zs, zr, ys, yr, ns, nr,
+    q_ref, k_ref, v_ref, dy_ref, gain_ref, seg_ref,
+    own, zin, yin, pre, scores, state_b, attn, gained, q_t, dattn, part_k, part_v,
+    norm_out, norm_in, loads, zs, zr, ys, yr, ns, nr,
 ):
     length = q_ref.shape[0]
     features = n_head * heads * HD
-    rows = HD // PARTS
-    chunks = heads * PARTS
+    parts = HD // rows
+    chunks = heads * parts
     s, h = lax.axis_index("seq"), lax.axis_index("head")
     y, z = lax.rem(s, INNER), s // INNER
     depth = n_seq // INNER
@@ -47,18 +49,44 @@
     def peer(k):
         return lax.rem(h + k, n_head)
 
+    def seq_peer(k):
+        return lax.rem(s + k, n_seq)
+
+    turns = sorted(range(1, n_seq), key=lambda k: abs(2 * k - n_seq))
+
+    fetches = [
+        pltpu.make_async_copy(src, dst, loads.at[i])
+        for i, (src, dst) in enumerate((
+            (k_hbm, k_ref), (v_hbm, v_ref), (q_hbm, q_ref), (dy_hbm, dy_ref),
+            (gain_hbm, gain_ref), (seg_hbm, seg_ref),
+        ))
+    ]
+    for fetch in fetches:
+        fetch.start()
+
     barrier = pltpu.get_barrier_semaphore()
-    pl.semaphore_signal(barrier, inc=1, device_id=(across, h), device_id_type=MESH)
+
+    def greet(device):
+        pl.semaphore_signal(barrier, inc=1, device_id=device, device_id_type=MESH)
+
     for k in range(1, n_head):
-        pl.semaphore_signal(barrier, inc=1, device_id=(s, peer(k)), device_id_type=MESH)
-
-    @pl.when(inner[0])
-    def _():
-        pl.semaphore_signal(barrier, inc=1, device_id=(s - INNER, h), device_id_type=MESH)
-
-    @pl.when(inner[1])
-    def _():
-        pl.semaphore_signal(barrier, inc=1, device_id=(s + INNER, h), device_id_type=MESH)
+        greet((s, peer(k)))
+    if direct:
+        for k in turns:
+            greet((seq_peer(k), h))
+        greetings = n_head - 1 + n_seq - 1
+    else:
+        greet((across, h))
+
+        @pl.when(inner[0])
+        def _():
+            greet((s - INNER, h))
+
+        @pl.when(inner[1])
+        def _():
+            greet((s + INNER, h))
+
+        greetings = n_head + inner[0].astype(jnp.int32) + inner[1].astype(jnp.int32)
 
     starts = (bottom, top)
     ends = (top, bottom)
@@ -78,8 +106,8 @@
         )
 
     def keep(p, i, term):
-        for j in range(PARTS):
-            own[p, i * PARTS + j] = term[j * rows:(j + 1) * rows]
+        for j in range(parts):
+            own[p, i * parts + j] = term[j * rows:(j + 1) * rows]
 
     def send_first(p):
         @pl.when(starts[p])
@@ -121,12 +149,16 @@
                     cross(p, c, own).start()
 
     def carried(p, i):
+        if direct:
+            pieces = [yin[p, i * parts + j] for j in range(parts)]
+            return jnp.concatenate(pieces, axis=0).astype(BF16)
+
         @pl.when(jnp.logical_not(starts[p] & gives_all[p]))
         def _():
-            for j in range(PARTS):
-                cross(p, i * PARTS + j, own).wait_recv()
-
-        pieces = [zin[p, i * PARTS + j] + yin[p, i * PARTS + j] for j in range(PARTS)]
+            for j in range(parts):
+                cross(p, i * parts + j, own).wait_recv()
+
+        pieces = [zin[p, i * parts + j] + yin[p, i * parts + j] for j in range(parts)]
         return jnp.concatenate(pieces, axis=0).astype(BF16)
 
     def drain(p):
@@ -139,13 +171,60 @@
             def _():
                 cross(p, c, own).wait_send()
 
+    def scatter(p, k, slot):
+        return pltpu.make_async_remote_copy(
+            src_ref=own.at[p, seq_peer(k)], dst_ref=zin.at[p, slot], send_sem=zs.at[p, k],
+            recv_sem=zr.at[p, slot], device_id=(seq_peer(k), h), device_id_type=MESH,
+        )
+
+    def give_back(p, k, slot):
+        return pltpu.make_async_remote_copy(
+            src_ref=pre.at[p, seq_peer(k)], dst_ref=yin.at[p, slot], send_sem=ys.at[p, k],
+            recv_sem=yr.at[p, slot], device_id=(seq_peer(k), h), device_id_type=MESH,
+        )
+
+    def begin(p):
+        if not direct:
+            send_first(p)
+            clear(p)
+            return
+        for k in turns:
+            scatter(p, k, s).start()
+        zin[p, s] = own[p, s]
+
+    def finish(p):
+        if not direct:
+            carry_on(p)
+            return
+        for k in turns:
+            scatter(p, k, seq_peer(k)).wait_recv()
+        total = jnp.zeros((rows, HD), F32)
+        for t in range(n_seq) if p == 0 else reversed(range(n_seq)):
+            pre[p, t] = total
+            total = total + zin[p, t]
+        for k in turns:
+            give_back(p, k, s).start()
+        yin[p, s] = pre[p, s]
+        for k in turns:
+            give_back(p, k, seq_peer(k)).wait_recv()
+
+    def settle(p):
+        if not direct:
+            drain(p)
+            return
+        for k in turns:
+            scatter(p, k, s).wait_send()
+            give_back(p, k, s).wait_send()
+
+    fetches[0].wait()
+    fetches[1].wait()
     for i in range(heads):
         keep(0, i, dot(k_ref[:, cols(i)], v_ref[:, cols(i)], TN))
 
-    pl.semaphore_wait(barrier, n_head + inner[0].astype(jnp.int32) + inner[1].astype(jnp.int32))
-    send_first(0)
-    clear(0)
-    clear(1)
+    pl.semaphore_wait(barrier, greetings)
+    begin(0)
+    for fetch in fetches[2:]:
+        fetch.wait()
 
     along = jnp.broadcast_to(seg_ref[...], (length, length))
     row_ids = lax.broadcasted_iota(jnp.int32, (length, length), 0)
@@ -155,8 +234,10 @@
         raw = dot(q_ref[:, cols(i)], k_ref[:, cols(i)], NT)
         scores[i] = jnp.where(allowed, raw, 0.0).astype(BF16)
         attn[:, cols(i)] = dot(scores[i], v_ref[:, cols(i)], NN)
-
-    carry_on(0)
+        gained[:, cols(i)] = gain_ref[:, cols(i)] * dy_ref[:, cols(i)].astype(F32)
+        q_t[i] = q_ref[:, cols(i)].T
+
+    finish(0)
 
     squares = jnp.zeros((length, HD), F32)
     products = jnp.zeros((length, HD), F32)
@@ -164,9 +245,8 @@
         state_b[i] = carried(0, i)
         flat = attn[:, cols(i)] + dot(q_ref[:, cols(i)], state_b[i], NN)
         attn[:, cols(i)] = flat
-        gained = gain_ref[:, cols(i)] * dy_ref[:, cols(i)].astype(F32)
         squares = squares + flat * flat
-        products = products + gained * flat
+        products = products + gained[:, cols(i)] * flat
 
     norm_out[0:1] = jnp.sum(squares.T, axis=0, keepdims=True)
     norm_out[1:2] = jnp.sum(products.T, axis=0, keepdims=True)
@@ -190,10 +270,9 @@
     beta = jnp.broadcast_to(beta_row, (HD, length)).T
 
     for i in range(heads):
-        gained = gain_ref[:, cols(i)] * dy_ref[:, cols(i)].astype(F32)
-        dattn[i] = (gained * inverse - attn[:, cols(i)] * beta).astype(BF16)
-        keep(1, i, dot(q_ref[:, cols(i)], dattn[i], TN))
-    send_first(1)
+        dattn[i] = (gained[:, cols(i)] * inverse - attn[:, cols(i)] * beta).astype(BF16)
+        keep(1, i, dot(q_t[i], dattn[i], NN))
+    begin(1)
 
     for i in range(heads):
         raw = dot(dattn[i], v_ref[:, cols(i)], NT)
@@ -205,7 +284,7 @@
         out = gain_ref[:, cols(i)] * attn[:, cols(i)] * inverse
         out_ref[:, cols(i)] = out.astype(BF16)
 
-    carry_on(1)
+    finish(1)
 
     for i in range(heads):
         later_b = carried(1, i)
@@ -214,46 +293,84 @@
         gv = part_v[i] + dot(k_ref[:, cols(i)], later_b, NN)
         gv_ref[:, cols(i)] = gv.astype(BF16)
 
-    drain(0)
-    drain(1)
+    settle(0)
+    settle(1)
     for k in range(1, n_head):
         share(k).wait_send()
+
+
+def write_out(*refs):
+    count = len(refs) // 2
+    copies = [
+        pltpu.make_async_copy(refs[i], refs[count + i], refs[-1].at[i]) for i in range(count)
+    ]
+    for copy in copies:
+        copy.start()
+    for copy in copies:
+        copy.wait()
 
 
 def on_device(n_seq, n_head, queries, keys, values, grad_out, gain, segment_ids):
     length, width = queries.shape
     heads = width // HD
-    chunks = heads * PARTS
+    rows = width // n_seq
+    direct = width % n_seq == 0 and rows % 8 == 0 and HD % rows == 0
+    if not direct:
+        rows = HD // PARTS
+    chunks = width // rows
     vmem = pl.BlockSpec(memory_space=pltpu.VMEM)
-    states = pltpu.VMEM((2, chunks, HD // PARTS, HD), F32)
-    return pl.pallas_call(
-        functools.partial(kernel, n_seq, n_head, heads),
+    hbm = pl.BlockSpec(memory_space=pl.ANY)
+    states = pltpu.VMEM((2, chunks, rows, HD), F32)
+    tokens = pltpu.VMEM((length, width), BF16)
+    wide = pltpu.VMEM((length, width), F32)
+    per_head = pltpu.VMEM((heads, length, HD), F32)
+    flags = pltpu.SemaphoreType.DMA((2, chunks))
+    results = pl.pallas_call(
+        functools.partial(kernel, n_seq, n_head, heads, direct, rows),
         out_shape=[jax.ShapeDtypeStruct((length, width), BF16)] * 4,
-        in_specs=[vmem] * 6,
+        in_specs=[hbm] * 6,
         out_specs=[vmem] * 4,
         scratch_shapes=[
+            tokens,
+            tokens,
+            tokens,
+            tokens,
+            pltpu.VMEM((1, width), F32),
+            pltpu.VMEM((1, length), jnp.int32),
+            states,
             states,
             states,
             states,
             pltpu.VMEM((heads, length, length), BF16),
             pltpu.VMEM((heads, HD, HD), BF16),
-            pltpu.VMEM((length, width), F32),
+            wide,
+            wide,
+            pltpu.VMEM((heads, HD, length), BF16),
             pltpu.VMEM((heads, length, HD), BF16),
-            pltpu.VMEM((heads, length, HD), F32),
-            pltpu.VMEM((heads, length, HD), F32),
+            per_head,
+            per_head,
             pltpu.VMEM((8, length), F32),
             pltpu.VMEM((n_head - 1, 8, length), F32),
-            pltpu.SemaphoreType.DMA((2, chunks)),
-            pltpu.SemaphoreType.DMA((2, chunks)),
-            pltpu.SemaphoreType.DMA((2, chunks)),
-            pltpu.SemaphoreType.DMA((2, chunks)),
+            pltpu.SemaphoreType.DMA((6,)),
+            flags,
+            flags,
+            flags,
+            flags,
             pltpu.SemaphoreType.DMA((n_head - 1,)),
             pltpu.SemaphoreType.DMA((n_head - 1,)),
         ],
         compiler_params=pltpu.CompilerParams(
-            collective_id=0, has_side_effects=True, vmem_limit_bytes=32 * 1024 * 1024
+            collective_id=0, has_side_effects=True, vmem_limit_bytes=VMEM
         ),
     )(queries, keys, values, grad_out, gain.reshape(1, width), segment_ids)
+    return pl.pallas_call(
+        write_out,
+        out_shape=[jax.ShapeDtypeStruct((length, width), BF16)] * 4,
+        in_specs=[hbm] * 4,
+        out_specs=[hbm] * 4,
+        scratch_shapes=[pltpu.SemaphoreType.DMA((4,))],
+        compiler_params=pltpu.CompilerParams(vmem_limit_bytes=VMEM),
+    )(*results)
 
 
 def solution(mesh):

time: 48 us -> 56.8 us (1.18)
  Pallas kernels: 39.6 us -> 56 us
  local copies, waits for them, and re-layouts: 7.57 us -> 0 us
    pallas_call x1 -> x2, Pallas kernels: 39.6 us -> 56 us  [the longest x1 39 us: on_device(): pl.pallas_call(functools.partial(kernel, n_seq, n_head, heads, direct, ro...]
    unnamed x16 -> x0, local copies, waits for them, and re-layouts: 7.57 us -> none
where the time goes in v2:
time: 56.8 us; the launch traced here: 56.7 us
  Pallas kernels  56 us (99%)
  between operations  0.64 us (1%)
    pallas_call x1, Pallas kernels, on_device(): pl.pallas_call(functools.partial(kernel, n_seq, n_head, heads, direct, ro...  39 us
    pallas_call x1, Pallas kernels, on_device(): pl.pallas_call(write_out, out_shape=[jax.ShapeDtypeStruct((length, width)...  17 us

profile of v2, /device:TPU:0, one launch (start us, length us, event | category | flops | bytes accessed | tf_op | source)
XLA Modules:
  0.0 56.7 jit_solution(16991726976675171535)
XLA Ops:
  0.6 39.0 %shard_map.93 = (bf16[128,512]{1,0:T(8,128)(2,1)}, bf16[128,512]{1,0:T(8,128)(2,1)}, bf16[128,512]{1,0:T(8,128)(2,1)}, bf16[128,512]{1,0:T(8,128)(2,1)}) custom-call(bf16[128,512]{1,0:T(8,128)(2,1)} %q_hbm.1, bf16[128,512]{1,0:T(8,128)(2,1)} %k_hbm.1, bf16[128,512]{1,0:T(8,128)(2,1)} %v_hbm.1, bf16[128,512]{1,0:T(8,128)(2,1)} %dy_hbm.1, f32[1,512]{1,0:T(1,128)} %bitcast.1, ...), custom_call_target="tpu_custom_call" | custom-call | tf_op jit(solution)/shard_map/pallas_call | solution.py:328
  39.7 17.0 %shard_map.94 = (bf16[128,512]{1,0:T(8,128)(2,1)}, bf16[128,512]{1,0:T(8,128)(2,1)}, bf16[128,512]{1,0:T(8,128)(2,1)}, bf16[128,512]{1,0:T(8,128)(2,1)}) custom-call(bf16[128,512]{1,0:T(8,128)(2,1)} %get-tuple-element.8.refs_0_, bf16[128,512]{1,0:T(8,128)(2,1)} %get-tuple-element.9.refs_1_, bf16[128,512]{1,0:T(8,128)(2,1)} %get-tuple-element.10.refs_2_, ...), custom_call_target="tpu_custom_call" | custom-call | tf_op jit(solution)/shard_map/pallas_call | solution.py:366

commit v3 on v1

--- a/solution.py
+++ b/solution.py
@@ -9,7 +9,8 @@
 
 HD = 128
 INNER = 2
-PARTS = 2
+PARTS = 4
+VMEM = 65000 * 1024
 MESH = pl.DeviceIdType.MESH
 F32 = jnp.float32
 BF16 = jnp.bfloat16
@@ -25,10 +26,12 @@
 
 
 def kernel(
-    n_seq, n_head, heads, q_ref, k_ref, v_ref, dy_ref, gain_ref, seg_ref,
+    n_seq, n_head, heads, q_hbm, k_hbm, v_hbm, dy_hbm, gain_hbm, seg_hbm,
+    out_hbm, gq_hbm, gk_hbm, gv_hbm,
     out_ref, gq_ref, gk_ref, gv_ref,
-    own, zin, yin, scores, state_b, attn, dattn, part_k, part_v, norm_out, norm_in,
-    zs, zr, ys, yr, ns, nr,
+    q_ref, k_ref, v_ref, dy_ref, gain_ref, seg_ref,
+    own, zin, yin, scores, state_b, attn, gained, q_t, dattn, part_k, part_v,
+    norm_out, norm_in, loads, stores, zs, zr, ys, yr, ns, nr,
 ):
     length = q_ref.shape[0]
     features = n_head * heads * HD
@@ -47,18 +50,40 @@
     def peer(k):
         return lax.rem(h + k, n_head)
 
+    fetches = [
+        pltpu.make_async_copy(src, dst, loads.at[i])
+        for i, (src, dst) in enumerate((
+            (k_hbm, k_ref), (v_hbm, v_ref), (q_hbm, q_ref), (dy_hbm, dy_ref),
+            (gain_hbm, gain_ref), (seg_hbm, seg_ref),
+        ))
+    ]
+    for fetch in fetches:
+        fetch.start()
+    writes = [
+        pltpu.make_async_copy(src, dst, stores.at[i])
+        for i, (src, dst) in enumerate((
+            (out_ref, out_hbm), (gq_ref, gq_hbm), (gk_ref, gk_hbm), (gv_ref, gv_hbm),
+        ))
+    ]
+
     barrier = pltpu.get_barrier_semaphore()
-    pl.semaphore_signal(barrier, inc=1, device_id=(across, h), device_id_type=MESH)
+
+    def greet(device):
+        pl.semaphore_signal(barrier, inc=1, device_id=device, device_id_type=MESH)
+
     for k in range(1, n_head):
-        pl.semaphore_signal(barrier, inc=1, device_id=(s, peer(k)), device_id_type=MESH)
+        greet((s, peer(k)))
+    greet((across, h))
 
     @pl.when(inner[0])
     def _():
-        pl.semaphore_signal(barrier, inc=1, device_id=(s - INNER, h), device_id_type=MESH)
+        greet((s - INNER, h))
 
     @pl.when(inner[1])
     def _():
-        pl.semaphore_signal(barrier, inc=1, device_id=(s + INNER, h), device_id_type=MESH)
+        greet((s + INNER, h))
+
+    greetings = n_head + inner[0].astype(jnp.int32) + inner[1].astype(jnp.int32)
 
     starts = (bottom, top)
     ends = (top, bottom)
@@ -81,10 +106,10 @@
         for j in range(PARTS):
             own[p, i * PARTS + j] = term[j * rows:(j + 1) * rows]
 
-    def send_first(p):
+    def send_first(p, chunk_ids):
         @pl.when(starts[p])
         def _():
-            for c in range(chunks):
+            for c in chunk_ids:
                 hop(p, c).start()
 
                 @pl.when(gives_all[p])
@@ -106,19 +131,19 @@
             for c in range(chunks):
                 hop(p, c).wait_recv()
 
+                own[p, c] = own[p, c] + zin[p, c]
+
+                @pl.when(jnp.logical_not(ends[p]))
+                def _():
+                    hop(p, c).start()
+
+                @pl.when(gives_all[p])
+                def _():
+                    cross(p, c, own).start()
+
                 @pl.when(jnp.logical_not(gives_all[p]))
                 def _():
                     cross(p, c, zin).start()
-
-                own[p, c] = own[p, c] + zin[p, c]
-
-                @pl.when(jnp.logical_not(ends[p]))
-                def _():
-                    hop(p, c).start()
-
-                @pl.when(gives_all[p])
-                def _():
-                    cross(p, c, own).start()
 
     def carried(p, i):
         @pl.when(jnp.logical_not(starts[p] & gives_all[p]))
@@ -139,13 +164,17 @@
             def _():
                 cross(p, c, own).wait_send()
 
+    fetches[0].wait()
+    fetches[1].wait()
     for i in range(heads):
         keep(0, i, dot(k_ref[:, cols(i)], v_ref[:, cols(i)], TN))
 
-    pl.semaphore_wait(barrier, n_head + inner[0].astype(jnp.int32) + inner[1].astype(jnp.int32))
-    send_first(0)
+    pl.semaphore_wait(barrier, greetings)
+    send_first(0, range(chunks))
     clear(0)
     clear(1)
+    for fetch in fetches[2:]:
+        fetch.wait()
 
     along = jnp.broadcast_to(seg_ref[...], (length, length))
     row_ids = lax.broadcasted_iota(jnp.int32, (length, length), 0)
@@ -155,6 +184,8 @@
         raw = dot(q_ref[:, cols(i)], k_ref[:, cols(i)], NT)
         scores[i] = jnp.where(allowed, raw, 0.0).astype(BF16)
         attn[:, cols(i)] = dot(scores[i], v_ref[:, cols(i)], NN)
+        gained[:, cols(i)] = gain_ref[:, cols(i)] * dy_ref[:, cols(i)].astype(F32)
+        q_t[i] = q_ref[:, cols(i)].T
 
     carry_on(0)
 
@@ -164,9 +195,8 @@
         state_b[i] = carried(0, i)
         flat = attn[:, cols(i)] + dot(q_ref[:, cols(i)], state_b[i], NN)
         attn[:, cols(i)] = flat
-        gained = gain_ref[:, cols(i)] * dy_ref[:, cols(i)].astype(F32)
         squares = squares + flat * flat
-        products = products + gained * flat
+        products = products + gained[:, cols(i)] * flat
 
     norm_out[0:1] = jnp.sum(squares.T, axis=0, keepdims=True)
     norm_out[1:2] = jnp.sum(products.T, axis=0, keepdims=True)
@@ -190,10 +220,9 @@
     beta = jnp.broadcast_to(beta_row, (HD, length)).T
 
     for i in range(heads):
-        gained = gain_ref[:, cols(i)] * dy_ref[:, cols(i)].astype(F32)
-        dattn[i] = (gained * inverse - attn[:, cols(i)] * beta).astype(BF16)
-        keep(1, i, dot(q_ref[:, cols(i)], dattn[i], TN))
-    send_first(1)
+        dattn[i] = (gained[:, cols(i)] * inverse - attn[:, cols(i)] * beta).astype(BF16)
+        keep(1, i, dot(q_t[i], dattn[i], NN))
+        send_first(1, range(i * PARTS, (i + 1) * PARTS))
 
     for i in range(heads):
         raw = dot(dattn[i], v_ref[:, cols(i)], NT)
@@ -205,6 +234,9 @@
         out = gain_ref[:, cols(i)] * attn[:, cols(i)] * inverse
         out_ref[:, cols(i)] = out.astype(BF16)
 
+    writes[0].start()
+    writes[1].start()
+
     carry_on(1)
 
     for i in range(heads):
@@ -214,46 +246,85 @@
         gv = part_v[i] + dot(k_ref[:, cols(i)], later_b, NN)
         gv_ref[:, cols(i)] = gv.astype(BF16)
 
+    writes[2].start()
+    writes[3].start()
     drain(0)
     drain(1)
     for k in range(1, n_head):
         share(k).wait_send()
+    for write in writes:
+        write.wait()
+
+
+def write_out(*refs):
+    sources, targets, held, come, go = refs[:4], refs[4:8], refs[8:12], refs[12], refs[13]
+    reads = [pltpu.make_async_copy(a, b, come.at[i]) for i, (a, b) in enumerate(zip(sources, held))]
+    writes = [pltpu.make_async_copy(a, b, go.at[i]) for i, (a, b) in enumerate(zip(held, targets))]
+    for read in reads:
+        read.start()
+    for read, write in zip(reads, writes):
+        read.wait()
+        write.start()
+    for write in writes:
+        write.wait()
 
 
 def on_device(n_seq, n_head, queries, keys, values, grad_out, gain, segment_ids):
     length, width = queries.shape
     heads = width // HD
     chunks = heads * PARTS
-    vmem = pl.BlockSpec(memory_space=pltpu.VMEM)
+    hbm = pl.BlockSpec(memory_space=pl.ANY)
     states = pltpu.VMEM((2, chunks, HD // PARTS, HD), F32)
-    return pl.pallas_call(
+    tokens = pltpu.VMEM((length, width), BF16)
+    wide = pltpu.VMEM((length, width), F32)
+    per_head = pltpu.VMEM((heads, length, HD), F32)
+    flags = pltpu.SemaphoreType.DMA((2, chunks))
+    results = pl.pallas_call(
         functools.partial(kernel, n_seq, n_head, heads),
         out_shape=[jax.ShapeDtypeStruct((length, width), BF16)] * 4,
-        in_specs=[vmem] * 6,
-        out_specs=[vmem] * 4,
-        scratch_shapes=[
+        in_specs=[hbm] * 6,
+        out_specs=[hbm] * 4,
+        scratch_shapes=[tokens] * 4 + [
+            tokens,
+            tokens,
+            tokens,
+            tokens,
+            pltpu.VMEM((1, width), F32),
+            pltpu.VMEM((1, length), jnp.int32),
             states,
             states,
             states,
             pltpu.VMEM((heads, length, length), BF16),
             pltpu.VMEM((heads, HD, HD), BF16),
-            pltpu.VMEM((length, width), F32),
+            wide,
+            wide,
+            pltpu.VMEM((heads, HD, length), BF16),
             pltpu.VMEM((heads, length, HD), BF16),
-            pltpu.VMEM((heads, length, HD), F32),
-            pltpu.VMEM((heads, length, HD), F32),
+            per_head,
+            per_head,
             pltpu.VMEM((8, length), F32),
             pltpu.VMEM((n_head - 1, 8, length), F32),
-            pltpu.SemaphoreType.DMA((2, chunks)),
-            pltpu.SemaphoreType.DMA((2, chunks)),
-            pltpu.SemaphoreType.DMA((2, chunks)),
-            pltpu.SemaphoreType.DMA((2, chunks)),
+            pltpu.SemaphoreType.DMA((6,)),
+            pltpu.SemaphoreType.DMA((4,)),
+            flags,
+            flags,
+            flags,
+            flags,
             pltpu.SemaphoreType.DMA((n_head - 1,)),
             pltpu.SemaphoreType.DMA((n_head - 1,)),
         ],
         compiler_params=pltpu.CompilerParams(
-            collective_id=0, has_side_effects=True, vmem_limit_bytes=32 * 1024 * 1024
+            collective_id=0, has_side_effects=True, vmem_limit_bytes=VMEM,
         ),
     )(queries, keys, values, grad_out, gain.reshape(1, width), segment_ids)
+    return pl.pallas_call(
+        write_out,
+        out_shape=[jax.ShapeDtypeStruct((length, width), BF16)] * 4,
+        in_specs=[hbm] * 4,
+        out_specs=[hbm] * 4,
+        scratch_shapes=[tokens] * 4 + [pltpu.SemaphoreType.DMA((4,))] * 2,
+        compiler_params=pltpu.CompilerParams(vmem_limit_bytes=VMEM),
+    )(*results)
 
 
 def solution(mesh):

time: 48 us -> 42.4 us (0.88)
  local copies, waits for them, and re-layouts: 7.57 us -> 0 us
  Pallas kernels: 39.6 us -> 41.6 us
    unnamed x16 -> x0, local copies, waits for them, and re-layouts: 7.57 us -> none
    pallas_call x0 -> x1, Pallas kernels: none -> 1.82 us  [on_device(): pl.pallas_call(write_out, out_shape=[jax.ShapeDtypeStruct((length, width)...]
where the time goes in v3:
time: 42.4 us; the launch traced here: 42.3 us
  Pallas kernels  41.6 us (98%)
  between operations  0.64 us (2%)
    pallas_call x1, Pallas kernels, on_device(): pl.pallas_call(functools.partial(kernel, n_seq, n_head, heads), out_shape...  39.8 us
    pallas_call x1, Pallas kernels, on_device(): pl.pallas_call(write_out, out_shape=[jax.ShapeDtypeStruct((length, width)...  1.82 us

profile of v3, /device:TPU:0, one launch (start us, length us, event | category | flops | bytes accessed | tf_op | source)
XLA Modules:
  0.0 42.3 jit_solution(5800784586277584019)
XLA Ops:
  0.6 39.8 %shard_map.93 = (bf16[128,512]{1,0:T(8,128)(2,1)}, bf16[128,512]{1,0:T(8,128)(2,1)}, bf16[128,512]{1,0:T(8,128)(2,1)}, bf16[128,512]{1,0:T(8,128)(2,1)}) custom-call(bf16[128,512]{1,0:T(8,128)(2,1)} %q_hbm.1, bf16[128,512]{1,0:T(8,128)(2,1)} %k_hbm.1, bf16[128,512]{1,0:T(8,128)(2,1)} %v_hbm.1, bf16[128,512]{1,0:T(8,128)(2,1)} %dy_hbm.1, f32[1,512]{1,0:T(1,128)} %bitcast.1, ...), custom_call_target="tpu_custom_call" | custom-call | tf_op jit(solution)/shard_map/pallas_call | solution.py:282
  40.4 1.8 %shard_map.94 = (bf16[128,512]{1,0:T(8,128)(2,1)}, bf16[128,512]{1,0:T(8,128)(2,1)}, bf16[128,512]{1,0:T(8,128)(2,1)}, bf16[128,512]{1,0:T(8,128)(2,1)}) custom-call(bf16[128,512]{1,0:T(8,128)(2,1)} %get-tuple-element.8.refs_0_, bf16[128,512]{1,0:T(8,128)(2,1)} %get-tuple-element.9.refs_1_, bf16[128,512]{1,0:T(8,128)(2,1)} %get-tuple-element.10.refs_2_, ...), custom_call_target="tpu_custom_call" | custom-call | tf_op jit(solution)/shard_map/pallas_call | solution.py:320

commit v4 on v3

--- a/solution.py
+++ b/solution.py
@@ -30,8 +30,8 @@
     out_hbm, gq_hbm, gk_hbm, gv_hbm,
     out_ref, gq_ref, gk_ref, gv_ref,
     q_ref, k_ref, v_ref, dy_ref, gain_ref, seg_ref,
-    own, zin, yin, scores, state_b, attn, gained, q_t, dattn, part_k, part_v,
-    norm_out, norm_in, loads, stores, zs, zr, ys, yr, ns, nr,
+    own, tot, zin, yin, raw_in, scores, state_b, attn, gained, q_t, dattn, part_k, part_v,
+    norm_out, norm_in, loads, stores, zs, zr, ys, yr, rs, rr, ns, nr,
 ):
     length = q_ref.shape[0]
     features = n_head * heads * HD
@@ -78,27 +78,36 @@
     @pl.when(inner[0])
     def _():
         greet((s - INNER, h))
+        greet((across - INNER, h))
 
     @pl.when(inner[1])
     def _():
         greet((s + INNER, h))
-
-    greetings = n_head + inner[0].astype(jnp.int32) + inner[1].astype(jnp.int32)
+        greet((across + INNER, h))
+
+    greetings = n_head + 2 * inner[0].astype(jnp.int32) + 2 * inner[1].astype(jnp.int32)
 
     starts = (bottom, top)
     ends = (top, bottom)
-    nexts = (s + INNER, s - INNER)
-    gives_all = (y == 0, y == 1)
-
-    def hop(p, c):
+    seconds = (z == 1, z == depth - 2)
+    steps = (INNER, -INNER)
+    takes_pair = (y == 1, y == 0)
+
+    def hop(p, c, src):
         return pltpu.make_async_remote_copy(
-            src_ref=own.at[p, c], dst_ref=zin.at[p, c], send_sem=zs.at[p, c],
-            recv_sem=zr.at[p, c], device_id=(nexts[p], h), device_id_type=MESH,
+            src_ref=src.at[p, c], dst_ref=zin.at[p, c], send_sem=zs.at[p, c],
+            recv_sem=zr.at[p, c], device_id=(s + steps[p], h), device_id_type=MESH,
         )
 
-    def cross(p, c, src):
+    def slant(p, c):
         return pltpu.make_async_remote_copy(
-            src_ref=src.at[p, c], dst_ref=yin.at[p, c], send_sem=ys.at[p, c],
+            src_ref=own.at[p, c], dst_ref=raw_in.at[p, c], send_sem=rs.at[p, c],
+            recv_sem=rr.at[p, c], device_id=(across + steps[p], h), device_id_type=MESH,
+        )
+
+    def cross(p, c):
+        return pltpu.make_async_remote_copy(
+            src_ref=own.at[p, c], dst_ref=yin.at[p, c], send_sem=ys.at[p, c],
             recv_sem=yr.at[p, c], device_id=(across, h), device_id_type=MESH,
         )
 
@@ -106,63 +115,62 @@
         for j in range(PARTS):
             own[p, i * PARTS + j] = term[j * rows:(j + 1) * rows]
 
-    def send_first(p, chunk_ids):
-        @pl.when(starts[p])
-        def _():
-            for c in chunk_ids:
-                hop(p, c).start()
-
-                @pl.when(gives_all[p])
+    def send_own(p, chunk_ids):
+        for c in chunk_ids:
+            cross(p, c).start()
+            if c < PARTS:
+                @pl.when(starts[p])
                 def _():
-                    cross(p, c, own).start()
-
-    def clear(p):
+                    hop(p, c, own).start()
+                    slant(p, c).start()
+
+    def carry_on(p):
         @pl.when(starts[p])
         def _():
             zin[p] = jnp.zeros(zin.shape[1:], F32)
-
-            @pl.when(gives_all[p])
-            def _():
-                yin[p] = jnp.zeros(yin.shape[1:], F32)
-
-    def carry_on(p):
+            for c in range(PARTS, chunks):
+                cross(p, c).wait_recv()
+                tot[p, c] = own[p, c] + yin[p, c]
+                hop(p, c, tot).start()
+            for c in range(PARTS):
+                cross(p, c).wait_recv()
+
         @pl.when(jnp.logical_not(starts[p]))
         def _():
             for c in range(chunks):
-                hop(p, c).wait_recv()
-
-                own[p, c] = own[p, c] + zin[p, c]
+                cross(p, c).wait_recv()
+                hop(p, c, tot).wait_recv()
+                if c < PARTS:
+                    @pl.when(seconds[p])
+                    def _():
+                        slant(p, c).wait_recv()
+                        zin[p, c] = zin[p, c] + raw_in[p, c]
 
                 @pl.when(jnp.logical_not(ends[p]))
                 def _():
-                    hop(p, c).start()
-
-                @pl.when(gives_all[p])
-                def _():
-                    cross(p, c, own).start()
-
-                @pl.when(jnp.logical_not(gives_all[p]))
-                def _():
-                    cross(p, c, zin).start()
+                    tot[p, c] = own[p, c] + yin[p, c] + zin[p, c]
+                    hop(p, c, tot).start()
 
     def carried(p, i):
-        @pl.when(jnp.logical_not(starts[p] & gives_all[p]))
-        def _():
-            for j in range(PARTS):
-                cross(p, i * PARTS + j, own).wait_recv()
-
-        pieces = [zin[p, i * PARTS + j] + yin[p, i * PARTS + j] for j in range(PARTS)]
+        pieces = [
+            zin[p, c] + jnp.where(takes_pair[p], yin[p, c], 0.0)
+            for c in range(i * PARTS, (i + 1) * PARTS)
+        ]
         return jnp.concatenate(pieces, axis=0).astype(BF16)
 
     def drain(p):
         for c in range(chunks):
-            @pl.when(jnp.logical_not(ends[p]))
-            def _():
-                hop(p, c).wait_send()
-
-            @pl.when(gives_all[p] | jnp.logical_not(starts[p]))
-            def _():
-                cross(p, c, own).wait_send()
+            cross(p, c).wait_send()
+
+        @pl.when(jnp.logical_not(ends[p]))
+        def _():
+            for c in range(chunks):
+                hop(p, c, tot).wait_send()
+
+        @pl.when(starts[p])
+        def _():
+            for c in range(PARTS):
+                slant(p, c).wait_send()
 
     fetches[0].wait()
     fetches[1].wait()
@@ -170,9 +178,7 @@
         keep(0, i, dot(k_ref[:, cols(i)], v_ref[:, cols(i)], TN))
 
     pl.semaphore_wait(barrier, greetings)
-    send_first(0, range(chunks))
-    clear(0)
-    clear(1)
+    send_own(0, range(chunks))
     for fetch in fetches[2:]:
         fetch.wait()
 
@@ -222,7 +228,7 @@
     for i in range(heads):
         dattn[i] = (gained[:, cols(i)] * inverse - attn[:, cols(i)] * beta).astype(BF16)
         keep(1, i, dot(q_t[i], dattn[i], NN))
-        send_first(1, range(i * PARTS, (i + 1) * PARTS))
+        send_own(1, range(i * PARTS, (i + 1) * PARTS))
 
     for i in range(heads):
         raw = dot(dattn[i], v_ref[:, cols(i)], NT)
@@ -294,6 +300,8 @@
             states,
             states,
             states,
+            states,
+            pltpu.VMEM((2, PARTS, HD // PARTS, HD), F32),
             pltpu.VMEM((heads, length, length), BF16),
             pltpu.VMEM((heads, HD, HD), BF16),
             wide,
@@ -310,6 +318,8 @@
             flags,
             flags,
             flags,
+            pltpu.SemaphoreType.DMA((2, PARTS)),
+            pltpu.SemaphoreType.DMA((2, PARTS)),
             pltpu.SemaphoreType.DMA((n_head - 1,)),
             pltpu.SemaphoreType.DMA((n_head - 1,)),
         ],

time: 42.4 us -> 43.7 us (1.031)
  Pallas kernels: 41.6 us -> 42.9 us
    pallas_call x1, Pallas kernels: 39.8 us -> 41 us  [on_device(): pl.pallas_call(functools.partial(kernel, n_seq, n_head, heads), out_shape...]
where the time goes in v4:
time: 43.7 us; the launch traced here: 43.5 us
  Pallas kernels  42.9 us (98%)
  between operations  0.64 us (1%)
    pallas_call x1, Pallas kernels, on_device(): pl.pallas_call(functools.partial(kernel, n_seq, n_head, heads), out_shape...  41 us
    pallas_call x1, Pallas kernels, on_device(): pl.pallas_call(write_out, out_shape=[jax.ShapeDtypeStruct((length, width)...  1.82 us

profile of v4, /device:TPU:0, one launch (start us, length us, event | category | flops | bytes accessed | tf_op | source)
XLA Modules:
  0.0 43.5 jit_solution(14039465474757332491)
XLA Ops:
  0.6 41.0 %shard_map.93 = (bf16[128,512]{1,0:T(8,128)(2,1)}, bf16[128,512]{1,0:T(8,128)(2,1)}, bf16[128,512]{1,0:T(8,128)(2,1)}, bf16[128,512]{1,0:T(8,128)(2,1)}) custom-call(bf16[128,512]{1,0:T(8,128)(2,1)} %q_hbm.1, bf16[128,512]{1,0:T(8,128)(2,1)} %k_hbm.1, bf16[128,512]{1,0:T(8,128)(2,1)} %v_hbm.1, bf16[128,512]{1,0:T(8,128)(2,1)} %dy_hbm.1, f32[1,512]{1,0:T(1,128)} %bitcast.1, ...), custom_call_target="tpu_custom_call" | custom-call | tf_op jit(solution)/shard_map/pallas_call | solution.py:288
  41.7 1.8 %shard_map.94 = (bf16[128,512]{1,0:T(8,128)(2,1)}, bf16[128,512]{1,0:T(8,128)(2,1)}, bf16[128,512]{1,0:T(8,128)(2,1)}, bf16[128,512]{1,0:T(8,128)(2,1)}) custom-call(bf16[128,512]{1,0:T(8,128)(2,1)} %get-tuple-element.8.refs_0_, bf16[128,512]{1,0:T(8,128)(2,1)} %get-tuple-element.9.refs_1_, bf16[128,512]{1,0:T(8,128)(2,1)} %get-tuple-element.10.refs_2_, ...), custom_call_target="tpu_custom_call" | custom-call | tf_op jit(solution)/shard_map/pallas_call | solution.py:330

commit v5 on v3

--- a/solution.py
+++ b/solution.py
@@ -30,13 +30,14 @@
     out_hbm, gq_hbm, gk_hbm, gv_hbm,
     out_ref, gq_ref, gk_ref, gv_ref,
     q_ref, k_ref, v_ref, dy_ref, gain_ref, seg_ref,
-    own, zin, yin, scores, state_b, attn, gained, q_t, dattn, part_k, part_v,
-    norm_out, norm_in, loads, stores, zs, zr, ys, yr, ns, nr,
+    own, tot, zin, yin, slant_in, scores, state_b, attn, gained, q_t, dattn, part_k, part_v,
+    norm_out, norm_in, loads, stores, zs, zr, ys, yr, rs, rr, ns, nr,
 ):
     length = q_ref.shape[0]
     features = n_head * heads * HD
     rows = HD // PARTS
     chunks = heads * PARTS
+    plain = chunks - PARTS
     s, h = lax.axis_index("seq"), lax.axis_index("head")
     y, z = lax.rem(s, INNER), s // INNER
     depth = n_seq // INNER
@@ -78,22 +79,30 @@
     @pl.when(inner[0])
     def _():
         greet((s - INNER, h))
+        greet((across - INNER, h))
 
     @pl.when(inner[1])
     def _():
         greet((s + INNER, h))
-
-    greetings = n_head + inner[0].astype(jnp.int32) + inner[1].astype(jnp.int32)
+        greet((across + INNER, h))
+
+    greetings = n_head + 2 * inner[0].astype(jnp.int32) + 2 * inner[1].astype(jnp.int32)
 
     starts = (bottom, top)
     ends = (top, bottom)
-    nexts = (s + INNER, s - INNER)
+    steps = (INNER, -INNER)
     gives_all = (y == 0, y == 1)
 
-    def hop(p, c):
+    def hop(p, c, src):
         return pltpu.make_async_remote_copy(
-            src_ref=own.at[p, c], dst_ref=zin.at[p, c], send_sem=zs.at[p, c],
-            recv_sem=zr.at[p, c], device_id=(nexts[p], h), device_id_type=MESH,
+            src_ref=src.at[p, c], dst_ref=zin.at[p, c], send_sem=zs.at[p, c],
+            recv_sem=zr.at[p, c], device_id=(s + steps[p], h), device_id_type=MESH,
+        )
+
+    def slant(p, c, src):
+        return pltpu.make_async_remote_copy(
+            src_ref=src.at[p, c], dst_ref=slant_in.at[p, c - plain], send_sem=rs.at[p, c - plain],
+            recv_sem=rr.at[p, c - plain], device_id=(across + steps[p], h), device_id_type=MESH,
         )
 
     def cross(p, c, src):
@@ -107,61 +116,97 @@
             own[p, i * PARTS + j] = term[j * rows:(j + 1) * rows]
 
     def send_first(p, chunk_ids):
-        @pl.when(starts[p])
-        def _():
-            for c in chunk_ids:
-                hop(p, c).start()
-
+        for c in chunk_ids:
+            @pl.when(starts[p])
+            def _():
+                hop(p, c, own).start()
+                if c >= plain:
+                    slant(p, c, own).start()
+                else:
+                    @pl.when(gives_all[p])
+                    def _():
+                        cross(p, c, own).start()
+
+            if c >= plain:
                 @pl.when(gives_all[p])
                 def _():
                     cross(p, c, own).start()
 
     def clear(p):
+        @pl.when(gives_all[p])
+        def _():
+            yin[p, plain:chunks] = jnp.zeros((PARTS, rows, HD), F32)
+
         @pl.when(starts[p])
         def _():
             zin[p] = jnp.zeros(zin.shape[1:], F32)
+            slant_in[p] = jnp.zeros(slant_in.shape[1:], F32)
 
             @pl.when(gives_all[p])
             def _():
-                yin[p] = jnp.zeros(yin.shape[1:], F32)
+                yin[p, 0:plain] = jnp.zeros((plain, rows, HD), F32)
 
     def carry_on(p):
         @pl.when(jnp.logical_not(starts[p]))
         def _():
             for c in range(chunks):
-                hop(p, c).wait_recv()
-
-                own[p, c] = own[p, c] + zin[p, c]
+                hop(p, c, tot).wait_recv()
+                tot[p, c] = own[p, c] + zin[p, c]
 
                 @pl.when(jnp.logical_not(ends[p]))
                 def _():
-                    hop(p, c).start()
-
-                @pl.when(gives_all[p])
-                def _():
-                    cross(p, c, own).start()
-
-                @pl.when(jnp.logical_not(gives_all[p]))
-                def _():
-                    cross(p, c, zin).start()
+                    hop(p, c, tot).start()
+                    if c >= plain:
+                        slant(p, c, tot).start()
+
+                if c < plain:
+                    @pl.when(gives_all[p])
+                    def _():
+                        cross(p, c, tot).start()
+
+                    @pl.when(jnp.logical_not(gives_all[p]))
+                    def _():
+                        cross(p, c, zin).start()
 
     def carried(p, i):
-        @pl.when(jnp.logical_not(starts[p] & gives_all[p]))
-        def _():
-            for j in range(PARTS):
-                cross(p, i * PARTS + j, own).wait_recv()
-
-        pieces = [zin[p, i * PARTS + j] + yin[p, i * PARTS + j] for j in range(PARTS)]
+        chunk_ids = range(i * PARTS, (i + 1) * PARTS)
+        if chunk_ids[0] < plain:
+            @pl.when(jnp.logical_not(starts[p] & gives_all[p]))
+            def _():
+                for c in chunk_ids:
+                    cross(p, c, own).wait_recv()
+
+            pieces = [zin[p, c] + yin[p, c] for c in chunk_ids]
+        else:
+            @pl.when(jnp.logical_not(gives_all[p]))
+            def _():
+                for c in chunk_ids:
+                    cross(p, c, own).wait_recv()
+
+            @pl.when(jnp.logical_not(starts[p]))
+            def _():
+                for c in chunk_ids:
+                    slant(p, c, own).wait_recv()
+
+            pieces = [zin[p, c] + yin[p, c] + slant_in[p, c - plain] for c in chunk_ids]
         return jnp.concatenate(pieces, axis=0).astype(BF16)
 
     def drain(p):
-        for c in range(chunks):
-            @pl.when(jnp.logical_not(ends[p]))
-            def _():
-                hop(p, c).wait_send()
-
-            @pl.when(gives_all[p] | jnp.logical_not(starts[p]))
-            def _():
+        @pl.when(jnp.logical_not(ends[p]))
+        def _():
+            for c in range(chunks):
+                hop(p, c, own).wait_send()
+                if c >= plain:
+                    slant(p, c, own).wait_send()
+
+        @pl.when(gives_all[p] | jnp.logical_not(starts[p]))
+        def _():
+            for c in range(plain):
+                cross(p, c, own).wait_send()
+
+        @pl.when(gives_all[p])
+        def _():
+            for c in range(plain, chunks):
                 cross(p, c, own).wait_send()
 
     fetches[0].wait()
@@ -294,6 +339,8 @@
             states,
             states,
             states,
+            states,
+            pltpu.VMEM((2, PARTS, HD // PARTS, HD), F32),
             pltpu.VMEM((heads, length, length), BF16),
             pltpu.VMEM((heads, HD, HD), BF16),
             wide,
@@ -310,6 +357,8 @@
             flags,
             flags,
             flags,
+            pltpu.SemaphoreType.DMA((2, PARTS)),
+            pltpu.SemaphoreType.DMA((2, PARTS)),
             pltpu.SemaphoreType.DMA((n_head - 1,)),
             pltpu.SemaphoreType.DMA((n_head - 1,)),
         ],

time: 42.4 us -> 43.2 us (1.019)
  Pallas kernels: 41.6 us -> 42.4 us
    pallas_call x1, Pallas kernels: 39.8 us -> 40.5 us  [on_device(): pl.pallas_call(functools.partial(kernel, n_seq, n_head, heads), out_shape...]
where the time goes in v5:
time: 43.2 us; the launch traced here: 43 us
  Pallas kernels  42.4 us (98%)
  between operations  0.64 us (1%)
    pallas_call x1, Pallas kernels, on_device(): pl.pallas_call(functools.partial(kernel, n_seq, n_head, heads), out_shape...  40.5 us
    pallas_call x1, Pallas kernels, on_device(): pl.pallas_call(write_out, out_shape=[jax.ShapeDtypeStruct((length, width)...  1.82 us

profile of v5, /device:TPU:0, one launch (start us, length us, event | category | flops | bytes accessed | tf_op | source)
XLA Modules:
  0.0 43.0 jit_solution(5388142156416787140)
XLA Ops:
  0.6 40.5 %shard_map.93 = (bf16[128,512]{1,0:T(8,128)(2,1)}, bf16[128,512]{1,0:T(8,128)(2,1)}, bf16[128,512]{1,0:T(8,128)(2,1)}, bf16[128,512]{1,0:T(8,128)(2,1)}) custom-call(bf16[128,512]{1,0:T(8,128)(2,1)} %q_hbm.1, bf16[128,512]{1,0:T(8,128)(2,1)} %k_hbm.1, bf16[128,512]{1,0:T(8,128)(2,1)} %v_hbm.1, bf16[128,512]{1,0:T(8,128)(2,1)} %dy_hbm.1, f32[1,512]{1,0:T(1,128)} %bitcast.1, ...), custom_call_target="tpu_custom_call" | custom-call | tf_op jit(solution)/shard_map/pallas_call | solution.py:327
  41.2 1.8 %shard_map.94 = (bf16[128,512]{1,0:T(8,128)(2,1)}, bf16[128,512]{1,0:T(8,128)(2,1)}, bf16[128,512]{1,0:T(8,128)(2,1)}, bf16[128,512]{1,0:T(8,128)(2,1)}) custom-call(bf16[128,512]{1,0:T(8,128)(2,1)} %get-tuple-element.8.refs_0_, bf16[128,512]{1,0:T(8,128)(2,1)} %get-tuple-element.9.refs_1_, bf16[128,512]{1,0:T(8,128)(2,1)} %get-tuple-element.10.refs_2_, ...), custom_call_target="tpu_custom_call" | custom-call | tf_op jit(solution)/shard_map/pallas_call | solution.py:369

commit v6 on v3

--- a/solution.py
+++ b/solution.py
@@ -9,7 +9,7 @@
 
 HD = 128
 INNER = 2
-PARTS = 4
+PARTS = 2
 VMEM = 65000 * 1024
 MESH = pl.DeviceIdType.MESH
 F32 = jnp.float32

time: 42.4 us -> 42.9 us (1.012)
  Pallas kernels: 41.6 us -> 42.1 us
    pallas_call x1, Pallas kernels: 39.8 us -> 40.3 us  [on_device(): pl.pallas_call(functools.partial(kernel, n_seq, n_head, heads), out_shape...]
where the time goes in v6:
time: 42.9 us; the launch traced here: 42.8 us
  Pallas kernels  42.1 us (98%)
  between operations  0.64 us (1%)
    pallas_call x1, Pallas kernels, on_device(): pl.pallas_call(functools.partial(kernel, n_seq, n_head, heads), out_shape...  40.3 us
    pallas_call x1, Pallas kernels, on_device(): pl.pallas_call(write_out, out_shape=[jax.ShapeDtypeStruct((length, width)...  1.82 us

profile of v6, /device:TPU:0, one launch (start us, length us, event | category | flops | bytes accessed | tf_op | source)
XLA Modules:
  0.0 42.8 jit_solution(18126836829434128738)
XLA Ops:
  0.6 40.3 %shard_map.93 = (bf16[128,512]{1,0:T(8,128)(2,1)}, bf16[128,512]{1,0:T(8,128)(2,1)}, bf16[128,512]{1,0:T(8,128)(2,1)}, bf16[128,512]{1,0:T(8,128)(2,1)}) custom-call(bf16[128,512]{1,0:T(8,128)(2,1)} %q_hbm.1, bf16[128,512]{1,0:T(8,128)(2,1)} %k_hbm.1, bf16[128,512]{1,0:T(8,128)(2,1)} %v_hbm.1, bf16[128,512]{1,0:T(8,128)(2,1)} %dy_hbm.1, f32[1,512]{1,0:T(1,128)} %bitcast.1, ...), custom_call_target="tpu_custom_call" | custom-call | tf_op jit(solution)/shard_map/pallas_call | solution.py:282
  41.0 1.8 %shard_map.94 = (bf16[128,512]{1,0:T(8,128)(2,1)}, bf16[128,512]{1,0:T(8,128)(2,1)}, bf16[128,512]{1,0:T(8,128)(2,1)}, bf16[128,512]{1,0:T(8,128)(2,1)}) custom-call(bf16[128,512]{1,0:T(8,128)(2,1)} %get-tuple-element.8.refs_0_, bf16[128,512]{1,0:T(8,128)(2,1)} %get-tuple-element.9.refs_1_, bf16[128,512]{1,0:T(8,128)(2,1)} %get-tuple-element.10.refs_2_, ...), custom_call_target="tpu_custom_call" | custom-call | tf_op jit(solution)/shard_map/pallas_call | solution.py:320
